TPU v7x, 512 devices: a whole 4x4x16 slice. The times are simulated.
512 devices in a mesh: phys: 2 (over x_hi), gx: 16 (over z), gy: 16 (over x_lo, y, core).
Axes of the slice: x: 4 (x_hi: 2, x_lo: 2; x = x_hi * 2 + x_lo), y: 4, z: 16, core: 2. Of those that a mesh axis runs over, the one named last changes fastest.
Arguments:
- models: float32 [2, 4, 1024, 2048], P('phys', None, 'gx', 'gy'), may hold values from -6 to 6
- channel_weight: float32 [2, 6], replicated, may hold values from 50 to 500
Outputs:
- gradient: float32 [2, 4, 1024, 2048], P('phys', None, 'gx', 'gy')
All inputs are finite; a program needn't handle non-finite values.
Results may differ from a plain program's by a relative error of at most 0.0001.
Values sent between devices are 32-bit elements; how exact they have to be, the bound alone decides.
No kernel may reach another device: no remote copies, remote signals or barrier semaphores. Data moves between devices by JAX's collectives and lax.ppermute only.
A program may use at most 64 MiB of HBM per device.

v0:
```python
import math
import jax
import jax.numpy as jnp
from jax import lax
from jax.sharding import PartitionSpec as P

gauss_total = sum((math.exp(-j * j / 50.0) for j in range(-15, 16)))


def extended(array, sides, width):
    for axis, dim in sides:
        peers, length = (lax.axis_size(axis), array.shape[dim])
        up = [(i, (i + 1) % peers) for i in range(peers - 1)]
        down = [(j, i) for i, j in up]
        last = lax.slice_in_dim(array, length - width, length, axis=dim)
        initial = lax.slice_in_dim(array, 0, width, axis=dim)
        before = lax.ppermute(last, axis, up)
        after = lax.ppermute(initial, axis, down)
        array = jnp.concatenate([before, array, after], axis=dim)
    return array


def from_partner(block, axis, stride):
    count = lax.axis_size(axis)
    route = []
    for low in range(count):
        high = low | 1 << stride
        if high != low and high < count:
            route += [(low, high), (high, low)]
    return lax.ppermute(block, axis, route)


def kernel_matrix(rows_n, cols_n, offset, dilation):
    row_index = lax.broadcasted_iota(jnp.int32, (rows_n, cols_n), 0)
    col_index = lax.broadcasted_iota(jnp.int32, (rows_n, cols_n), 1)
    distance = row_index - col_index + offset
    tap_index = distance // dilation
    on_tap = (distance == tap_index * dilation) & (jnp.abs(tap_index) <= 15)
    tap_float = tap_index.astype(jnp.float32)
    weights = jnp.exp(-tap_float * tap_float / 50.0) / gauss_total
    return jnp.where(on_tap, weights, 0.0)


def smooth_middle(values, dilation):
    lead, length, trail = values.shape
    highest = lax.Precision.HIGHEST
    if length <= 256:
        return jnp.einsum(
            "ij,ajb->aib", kernel_matrix(length, length, 0, dilation), values, precision=highest
        )
    block_count = length // 128
    blocks = values.reshape(lead, block_count, 128, trail)
    zero_block = jnp.zeros((lead, 1, 128, trail), values.dtype)
    after_blocks = jnp.concatenate([blocks[:, 1:], zero_block], 1)
    before_blocks = jnp.concatenate([zero_block, blocks[:, :-1]], 1)
    result = jnp.einsum(
        "ij,anjb->anib", kernel_matrix(128, 128, 0, dilation), blocks, precision=highest
    )
    result = result + jnp.einsum(
        "ij,anjb->anib", kernel_matrix(128, 128, -128, dilation), after_blocks, precision=highest
    )
    result = result + jnp.einsum(
        "ij,anjb->anib", kernel_matrix(128, 128, 128, dilation), before_blocks, precision=highest
    )
    return result.reshape(lead, length, trail)


def smooth_last(values, dilation):
    lead, trail, length = values.shape
    highest = lax.Precision.HIGHEST
    block_count = length // 128
    blocks = values.reshape(lead, trail, block_count, 128)
    zero_block = jnp.zeros((lead, trail, 1, 128), values.dtype)
    after_blocks = jnp.concatenate([blocks[:, :, 1:], zero_block], 2)
    before_blocks = jnp.concatenate([zero_block, blocks[:, :, :-1]], 2)
    result = jnp.einsum(
        "ajnk,ik->ajni", blocks, kernel_matrix(128, 128, 0, dilation), precision=highest
    )
    result = result + jnp.einsum(
        "ajnk,ik->ajni", after_blocks, kernel_matrix(128, 128, -128, dilation), precision=highest
    )
    result = result + jnp.einsum(
        "ajnk,ik->ajni", before_blocks, kernel_matrix(128, 128, 128, dilation), precision=highest
    )
    return result.reshape(lead, trail, length)


def smooth_rows(row_stack):
    row_count, x_cells, y_cells = row_stack.shape
    half_rows = row_count // 2
    depth_cells = row_count // 12
    z_rows = row_stack.reshape(12, depth_cells, x_cells * y_cells)
    z_done = jnp.concatenate([smooth_middle(z_rows[:6], 1), smooth_middle(z_rows[6:], 4)], 0)
    z_done = z_done.reshape(row_count, x_cells, y_cells)
    per_device = row_count // lax.axis_size("gx")
    dilation = jnp.where(lax.axis_index("gx") * per_device >= half_rows, 4, 1)
    x_done = lax.all_to_all(
        smooth_middle(
            lax.all_to_all(z_done, "gx", split_axis=0, concat_axis=1, tiled=True), dilation
        ),
        "gx",
        split_axis=1,
        concat_axis=0,
        tiled=True,
    )
    per_column = row_count // lax.axis_size("gy")
    dilation = jnp.where(lax.axis_index("gy") * per_column >= half_rows, 4, 1)
    return lax.all_to_all(
        smooth_last(
            lax.all_to_all(x_done, "gy", split_axis=0, concat_axis=2, tiled=True), dilation
        ),
        "gy",
        split_axis=2,
        concat_axis=0,
        tiled=True,
    )


def shards(models, channel_weight):
    model_field = models[0]
    depth_cells, x_cells, y_cells = model_field.shape
    padded = extended(model_field, (("gx", 1), ("gy", 2)), 1)
    z_padded = jnp.pad(model_field, ((1, 1), (0, 0), (0, 0)))
    slope_x = 0.5 * (padded[:, 2:, 1:-1] - padded[:, :-2, 1:-1])
    slope_y = 0.5 * (padded[:, 1:-1, 2:] - padded[:, 1:-1, :-2])
    slope_z = 0.5 * (z_padded[2:] - z_padded[:-2])
    tensor = jnp.stack(
        [
            slope_x * slope_x,
            slope_y * slope_y,
            slope_z * slope_z,
            slope_x * slope_y,
            slope_x * slope_z,
            slope_y * slope_z,
        ],
        0,
    )
    row_stack = jnp.concatenate([tensor, tensor], 0).reshape(12 * depth_cells, x_cells, y_cells)
    smoothed = smooth_rows(row_stack)
    partner_part = from_partner(smoothed, "phys", 0)
    weights = jnp.repeat(channel_weight.reshape(12), depth_cells)[:, None, None]
    adjoint = smooth_rows((smoothed - partner_part) * weights)
    half_rows = 6 * depth_cells
    combined = (adjoint[:half_rows] + adjoint[half_rows:]).reshape(6, depth_cells, x_cells, y_cells)
    q_x = 2.0 * combined[0] * slope_x + combined[3] * slope_y + combined[4] * slope_z
    q_y = 2.0 * combined[1] * slope_y + combined[3] * slope_x + combined[5] * slope_z
    q_z = 2.0 * combined[2] * slope_z + combined[4] * slope_x + combined[5] * slope_y
    lateral = extended(jnp.stack([q_x, q_y], 0), (("gx", 2), ("gy", 3)), 1)
    pad_z = jnp.pad(q_z, ((1, 1), (0, 0), (0, 0)))
    result = 0.5 * (lateral[0, :, :-2, 1:-1] - lateral[0, :, 2:, 1:-1])
    result = result + 0.5 * (lateral[1, :, 1:-1, :-2] - lateral[1, :, 1:-1, 2:])
    result = result + 0.5 * (pad_z[:-2] - pad_z[2:])
    return result[None]


def solution(mesh):
    in_specs = (P("phys", None, "gx", "gy"), P())
    out_specs = P("phys", None, "gx", "gy")
    return jax.shard_map(shards, mesh=mesh, in_specs=in_specs, out_specs=out_specs, check_vma=False)
```

profile of v0, /device:TPU:25, one launch (start us, length us, event | category | flops | bytes accessed | tf_op | source)
XLA Modules:
  0.0 646.8 jit_solution(4827848419836089784)
XLA Ops:
  2.1 4.2 collective-permute-start.1
  8.0 3.5 collective-permute-start.2
  11.6 4.1 collective-permute-start.3
  25.3 16.5 %all-to-all-start = ((f32[48,64,128]{2,1,0:T(8,128)}), f32[48,64,128]{2,1,0:T(8,128)S(1)}, u32[]{:S(2)}, u32[]{:S(2)}) async-start(f32[48,64,128]{2,1,0:T(8,128)} %reshape.70), calls=%async_computation | async-start | bytes 3145728 | tf_op jit(solution)/shard_map/all_to_all | solution.py:99
  41.8 68.9 %all-to-all-done = f32[48,64,128]{2,1,0:T(8,128)S(1)} async-done(((f32[48,64,128]{2,1,0:T(8,128)}), f32[48,64,128]{2,1,0:T(8,128)S(1)}, u32[]{:S(2)}, u32[]{:S(2)}) %all-to-all-start) | async-done | bytes 1572896 | tf_op jit(solution)/shard_map/all_to_all | solution.py:99
  115.0 2.3 add_add_fusion.3
  118.4 101.6 %all_to_all.129 = f32[3,1024,128]{2,0,1:T(4,128)S(1)} all-to-all(f32[3,1024,128]{2,0,1:T(4,128)S(1)} %copy.22), channel_id=1, replica_groups=mesh['phys'=2,'gx'=16,'gy'=16] {'gx'}, dimensions={1} | all-to-all | bytes 3145728 | tf_op jit(solution)/shard_map/all_to_all | solution.py:97
  221.5 12.1 %all-to-all-start.2 = ((f32[48,64,128]{2,1,0:T(8,128)}), f32[48,64,128]{2,1,0:T(8,128)S(1)}, u32[]{:S(2)}, u32[]{:S(2)}) async-start(f32[48,64,128]{2,1,0:T(8,128)} %bitcast.19), calls=%async_computation.2 | async-start | bytes 3145728 | tf_op jit(solution)/shard_map/all_to_all | solution.py:110
  233.6 22.0 %all-to-all-done.2 = f32[48,64,128]{2,1,0:T(8,128)S(1)} async-done(((f32[48,64,128]{2,1,0:T(8,128)}), f32[48,64,128]{2,1,0:T(8,128)S(1)}, u32[]{:S(2)}, u32[]{:S(2)}) %all-to-all-start.2) | async-done | bytes 1572896 | tf_op jit(solution)/shard_map/all_to_all | solution.py:110
  256.8 2.9 fusion.98
  264.0 2.7 copy.41
  266.7 5.4 reshape.87
  272.1 24.6 %all_to_all.130 = f32[16,1,24576]{2,1,0:T(1,128)S(1)} all-to-all(f32[16,1,24576]{2,1,0:T(1,128)S(1)} %reshape.87), channel_id=1, replica_groups=mesh['phys'=2,'gx'=16,'gy'=16] {'gy'}, dimensions={0} | all-to-all | bytes 3145728 | tf_op jit(solution)/shard_map/all_to_all | solution.py:108
  297.2 4.4 reduce
  301.7 3.7 reshape.88
  305.4 3.3 copy.27
  308.7 4.6 collective-permute-start.4
  315.4 32.5 %collective-permute-done.4 = f32[48,64,128]{2,1,0:T(8,128)S(1)} collective-permute-done((f32[48,64,128]{2,1,0:T(8,128)S(1)}, f32[48,64,128]{2,1,0:T(8,128)S(1)}, u32[]{:S(2)}, u32[]{:S(2)}) %collective-permute-start.4) | collective-permute-done | bytes 1572896 | tf_op jit(solution)/shard_map/ppermute | solution.py:30
  354.0 73.7 %all_to_all.131 = f32[48,64,128]{2,1,0:T(8,128)S(1)} all-to-all(f32[48,64,128]{2,1,0:T(8,128)S(1)} %reshape.75), channel_id=1, replica_groups=mesh['phys'=2,'gx'=16,'gy'=16] {'gx'}, dimensions={0} | all-to-all | bytes 3145728 | tf_op jit(solution)/shard_map/all_to_all | solution.py:99
  435.5 102.2 %all_to_all.132 = f32[3,1024,128]{2,0,1:T(4,128)S(1)} all-to-all(f32[3,1024,128]{2,0,1:T(4,128)S(1)} %copy.29), channel_id=1, replica_groups=mesh['phys'=2,'gx'=16,'gy'=16] {'gx'}, dimensions={1} | all-to-all | bytes 3145728 | tf_op jit(solution)/shard_map/all_to_all | solution.py:97
  537.9 31.8 %all_to_all.133 = f32[48,64,128]{2,1,0:T(8,128)S(1)} all-to-all(f32[48,64,128]{2,1,0:T(8,128)S(1)} %bitcast.139), channel_id=1, replica_groups=mesh['phys'=2,'gx'=16,'gy'=16] {'gy'}, dimensions={0} | all-to-all | bytes 3145728 | tf_op jit(solution)/shard_map/all_to_all | solution.py:110
  570.6 2.9 fusion.96
  578.2 2.7 copy.42
  580.9 5.4 reshape.89
  586.3 24.9 %all_to_all.134 = f32[16,1,24576]{2,1,0:T(1,128)S(1)} all-to-all(f32[16,1,24576]{2,1,0:T(1,128)S(1)} %reshape.89), channel_id=1, replica_groups=mesh['phys'=2,'gx'=16,'gy'=16] {'gy'}, dimensions={0} | all-to-all | bytes 3145728 | tf_op jit(solution)/shard_map/all_to_all | solution.py:108
  611.2 4.4 reduce.1
  615.6 3.7 reshape.90
  619.3 2.8 slice_add_fusion
  622.9 2.7 collective-permute-start.5
  627.0 3.0 collective-permute-done.6
  630.2 5.4 collective-permute-start.7
  639.2 6.5 %collective-permute-done.8 = f32[2,4,66,1]{3,2,1,0:T(8,128)S(1)} collective-permute-done((f32[2,4,66,1]{3,2,1,0:T(8,128)S(1)}, f32[2,4,66,1]{3,2,1,0:T(8,128)S(1)}, u32[]{:S(2)}, u32[]{:S(2)}) %collective-permute-start.8) | collective-permute-done | bytes 2144 | tf_op jit(solution)/shard_map/ppermute | solution.py:18
  (74 shorter events, 54.4 us)
Async XLA Ops:
  0.0 19.1 %copy-start = (f32[1,4,64,128]{3,2,1,0:T(8,128)S(1)}, f32[1,4,64,128]{3,2,1,0:T(8,128)}, u32[]{:S(2)}) copy-start(f32[1,4,64,128]{3,2,1,0:T(8,128)} %param.2) | copy-start | bytes 393220
  0.8 5.5 collective-permute-start
  2.1 4.9 collective-permute-start.1
  8.0 8.6 %collective-permute-start.2 = (f32[4,66,1]{2,1,0:T(8,128)S(1)}, f32[4,66,1]{2,1,0:T(8,128)S(1)}, u32[]{:S(2)}, u32[]{:S(2)}) collective-permute-start(f32[4,66,1]{2,1,0:T(8,128)S(1)} %get-tuple-element.24), channel_id=1, source_target_pairs={{1,0},{2,1},{3,2},{4,3},{5,4},{6,5},{7,6},{8,7},{9,8},{10,9},{11,1... | collective-permute-start | bytes 3176 | tf_op jit(solution)/shard_map/ppermute | solution.py:18
  11.6 6.2 collective-permute-start.3
  25.3 85.4 %all-to-all-start = ((f32[48,64,128]{2,1,0:T(8,128)}), f32[48,64,128]{2,1,0:T(8,128)S(1)}, u32[]{:S(2)}, u32[]{:S(2)}) async-start(f32[48,64,128]{2,1,0:T(8,128)} %reshape.70), calls=%async_computation | async-start | bytes 3145728 | tf_op jit(solution)/shard_map/all_to_all | solution.py:99
  221.5 34.1 %all-to-all-start.2 = ((f32[48,64,128]{2,1,0:T(8,128)}), f32[48,64,128]{2,1,0:T(8,128)S(1)}, u32[]{:S(2)}, u32[]{:S(2)}) async-start(f32[48,64,128]{2,1,0:T(8,128)} %bitcast.19), calls=%async_computation.2 | async-start | bytes 3145728 | tf_op jit(solution)/shard_map/all_to_all | solution.py:110
  305.3 7.9 %copy-start.1 = (f32[2,6]{1,0:T(2,128)S(1)}, f32[2,6]{1,0:T(2,128)}, u32[]{:S(2)}) copy-start(f32[2,6]{1,0:T(2,128)} %param.3) | copy-start | bytes 148
  308.7 39.2 %collective-permute-start.4 = (f32[48,64,128]{2,1,0:T(8,128)S(1)}, f32[48,64,128]{2,1,0:T(8,128)S(1)}, u32[]{:S(2)}, u32[]{:S(2)}) collective-permute-start(f32[48,64,128]{2,1,0:T(8,128)S(1)} %bitcast.133), channel_id=1, source_target_pairs={{0,256},{256,0},{1,257},{257,1},{2,258},{258,2},{3,259},{259,3},{4... | collective-permute-start | bytes 4718600 | tf_op jit(solution)/shard_map/ppermute | solution.py:30
  622.9 4.0 collective-permute-start.5
  625.6 4.4 collective-permute-start.6
  630.2 9.1 %collective-permute-start.7 = (f32[2,4,66,1]{3,2,1,0:T(8,128)S(1)}, f32[2,4,66,1]{3,2,1,0:T(8,128)S(1)}, u32[]{:S(2)}, u32[]{:S(2)}) collective-permute-start(f32[2,4,66,1]{3,2,1,0:T(8,128)S(1)} %get-tuple-element.16), channel_id=1, source_target_pairs={{0,1},{1,2},{2,3},{3,4},{4,5},{5,6},{6,7},{7,8},{8,9},{9,10},{10,1... | collective-permute-start | bytes 6344 | tf_op jit(solution)/shard_map/ppermute | solution.py:17
  635.6 10.2 %collective-permute-start.8 = (f32[2,4,66,1]{3,2,1,0:T(8,128)S(1)}, f32[2,4,66,1]{3,2,1,0:T(8,128)S(1)}, u32[]{:S(2)}, u32[]{:S(2)}) collective-permute-start(f32[2,4,66,1]{3,2,1,0:T(8,128)S(1)} %get-tuple-element.17), channel_id=1, source_target_pairs={{1,0},{2,1},{3,2},{4,3},{5,4},{6,5},{7,6},{8,7},{9,8},{10,9},{11,1... | collective-permute-start | bytes 6344 | tf_op jit(solution)/shard_map/ppermute | solution.py:18
where the time goes:
time: 652 us; the launch traced here: 647 us
  blocking collectives  359 us (55%)
  waiting for transfers between devices  137 us (21%)
  starting transfers between devices  57.6 us (9%)
  local copies, waits for them, and re-layouts  42.1 us (6%)
  matrix products  33.3 us (5%)
  other arithmetic  16.6 us (3%)
    all_to_all x2, blocking collectives, smooth_rows(): lax.all_to_all(smooth_middle(lax.all_to_all(z_done, 'gx', split_axis=0, c...  204 us
    all_to_all x1, blocking collectives, smooth_rows(): lax.all_to_all(z_done, 'gx', split_axis=0, concat_axis=1, tiled=True)  73.7 us
    all_to_all x1, waiting for transfers between devices, smooth_rows(): lax.all_to_all(z_done, 'gx', split_axis=0, concat_axis=1, tiled=True)  68.9 us
    all_to_all x2, blocking collectives, smooth_rows(): lax.all_to_all(smooth_last(lax.all_to_all(x_done, 'gy', split_axis=0, con...  49.4 us
    ppermute x1, waiting for transfers between devices, from_partner(): return lax.ppermute(block, axis, route)  32.5 us
    all_to_all x1, blocking collectives, smooth_rows(): lax.all_to_all(x_done, 'gy', split_axis=0, concat_axis=2, tiled=True)  31.8 us
    all_to_all x1, waiting for transfers between devices, smooth_rows(): lax.all_to_all(x_done, 'gy', split_axis=0, concat_axis=2, tiled=True)  22 us
    unnamed x13, local copies, waits for them, and re-layouts  18.4 us
  transfers between devices with their start and end apart: 11, of which 9 were waited for; matrix products, arithmetic and copies ran while one was open for 0% of the time, Pallas kernels for 0%

commit v1 on v0

--- a/solution.py
+++ b/solution.py
@@ -5,6 +5,39 @@
 from jax.sharding import PartitionSpec as P
 
 gauss_total = sum((math.exp(-j * j / 50.0) for j in range(-15, 16)))
+
+
+def _mix_cells(field, dim_no, own_rows):
+    z1, mat_out = (field.shape[:dim_no], field.shape[dim_no + 1 :])
+    spare = jnp.moveaxis(field.reshape(*z1, own_rows, -1, *mat_out), dim_no, 0)
+    return spare
+
+
+def direct_rates_on_mesh(inner_x, out_dim):
+    inner_x = jnp.moveaxis(inner_x, 0, out_dim)
+    ready = inner_x.shape
+    oldest = inner_x.reshape(
+        *ready[:out_dim], ready[out_dim] * ready[out_dim + 1], *ready[out_dim + 2 :]
+    )
+    return oldest
+
+
+def begin_the_notes(v0, named_axis, arr, field_in):
+    part_now, local_now = (lax.axis_size(named_axis), lax.axis_index(named_axis))
+    formed = _mix_cells(v0, arr, part_now)
+    lanes = [formed[local_now]]
+    for hop_no in range(1, part_now):
+        h_now = formed[(local_now + hop_no) % part_now]
+        lanes.append(
+            lax.ppermute(
+                h_now,
+                axis_name=named_axis,
+                perm=[(dd, (dd + hop_no) % part_now) for dd in range(part_now)],
+            )
+        )
+    formed = jnp.stack(lanes, axis=0)[(local_now - jnp.arange(part_now)) % part_now]
+    carry_out = direct_rates_on_mesh(formed, field_in)
+    return carry_out
 
 
 def extended(array, sides, width):
@@ -94,14 +127,13 @@
     z_done = z_done.reshape(row_count, x_cells, y_cells)
     per_device = row_count // lax.axis_size("gx")
     dilation = jnp.where(lax.axis_index("gx") * per_device >= half_rows, 4, 1)
-    x_done = lax.all_to_all(
+    x_done = begin_the_notes(
         smooth_middle(
             lax.all_to_all(z_done, "gx", split_axis=0, concat_axis=1, tiled=True), dilation
         ),
         "gx",
-        split_axis=1,
-        concat_axis=0,
-        tiled=True,
+        1,
+        0,
     )
     per_column = row_count // lax.axis_size("gy")
     dilation = jnp.where(lax.axis_index("gy") * per_column >= half_rows, 4, 1)

time: 652 us -> 665 us (1.020)
  blocking collectives: 359 us -> 150 us
  starting transfers between devices: 57.6 us -> 209 us
  waiting for transfers between devices: 137 us -> 207 us
    all_to_all x2 -> x0, blocking collectives: 204 us -> none  [smooth_rows(): lax.all_to_all(smooth_middle(lax.all_to_all(z_done, 'gx', split_axis=0, c...]
    ppermute x0 -> x30, starting transfers between devices: none -> 158 us  [begin_the_notes(): lax.ppermute(h_now, axis_name=named_axis, perm=[(dd, (dd + hop_no) % part...]
    ppermute x0 -> x30, waiting for transfers between devices: none -> 69.5 us  [begin_the_notes(): lax.ppermute(h_now, axis_name=named_axis, perm=[(dd, (dd + hop_no) % part...]
    unnamed x13 -> x45, local copies, waits for them, and re-layouts: 18.4 us -> 18.7 us
  transfers between devices with their start and end apart: 11 -> 41, of which waited for: 9 -> 22; matrix products, arithmetic and copies ran while one was open for 0% -> 0% of each run, Pallas kernels for 0% -> 0%
where the time goes in v1:
time: 665 us; the launch traced here: 659 us
  starting transfers between devices  209 us (31%)
  waiting for transfers between devices  207 us (31%)
  blocking collectives  150 us (23%)
  local copies, waits for them, and re-layouts  41.5 us (6%)
  matrix products  33.2 us (5%)
  other arithmetic  16.4 us (2%)
    ppermute x30, starting transfers between devices, begin_the_notes(): lax.ppermute(h_now, axis_name=named_axis, perm=[(dd, (dd + hop_no) % part...  158 us
    all_to_all x1, blocking collectives, smooth_rows(): lax.all_to_all(z_done, 'gx', split_axis=0, concat_axis=1, tiled=True)  74.2 us
    ppermute x30, waiting for transfers between devices, begin_the_notes(): lax.ppermute(h_now, axis_name=named_axis, perm=[(dd, (dd + hop_no) % part...  69.5 us
    all_to_all x1, waiting for transfers between devices, smooth_rows(): lax.all_to_all(z_done, 'gx', split_axis=0, concat_axis=1, tiled=True)  68.7 us
    all_to_all x2, blocking collectives, smooth_rows(): lax.all_to_all(smooth_last(lax.all_to_all(x_done, 'gy', split_axis=0, con...  49.4 us
    ppermute x1, waiting for transfers between devices, from_partner(): return lax.ppermute(block, axis, route)  32.6 us
    all_to_all x1, blocking collectives, smooth_rows(): lax.all_to_all(x_done, 'gy', split_axis=0, concat_axis=2, tiled=True)  26.4 us
    all_to_all x1, waiting for transfers between devices, smooth_rows(): lax.all_to_all(x_done, 'gy', split_axis=0, concat_axis=2, tiled=True)  22 us
  transfers between devices with their start and end apart: 41, of which 22 were waited for; matrix products, arithmetic and copies ran while one was open for 0% of the time, Pallas kernels for 0%

profile of v1, /device:TPU:25, one launch (start us, length us, event | category | flops | bytes accessed | tf_op | source)
XLA Modules:
  0.0 658.8 jit_solution(1457150500149314450)
XLA Ops:
  25.3 16.5 %all-to-all-start = ((f32[48,64,128]{2,1,0:T(8,128)}), f32[48,64,128]{2,1,0:T(8,128)S(1)}, u32[]{:S(2)}, u32[]{:S(2)}) async-start(f32[48,64,128]{2,1,0:T(8,128)} %reshape.181), calls=%async_computation | async-start | bytes 3145728 | tf_op jit(solution)/shard_map/all_to_all | solution.py:132
  42.0 68.7 %all-to-all-done = f32[48,64,128]{2,1,0:T(8,128)S(1)} async-done(((f32[48,64,128]{2,1,0:T(8,128)}), f32[48,64,128]{2,1,0:T(8,128)S(1)}, u32[]{:S(2)}, u32[]{:S(2)}) %all-to-all-start) | async-done | bytes 1572896 | tf_op jit(solution)/shard_map/all_to_all | solution.py:132
  125.1 6.0 collective-permute-start.6
  131.0 6.1 collective-permute-start.7
  139.1 8.5 %collective-permute-start.9 = (f32[3,64,128]{2,1,0:T(8,128)S(1)}, f32[3,64,128]{2,1,0:T(8,128)S(1)}, u32[]{:S(2)}, u32[]{:S(2)}) collective-permute-start(f32[3,64,128]{2,1,0:T(8,128)S(1)} %get-tuple-element.38), channel_id=1, source_target_pairs={{0,96},{16,112},{32,128},{48,144},{64,160},{80,176},{96,192},{112,... | collective-permute-start | bytes 294920 | tf_op jit(solution)/shard_map/ppermute | solution.py:32
  147.6 5.5 collective-permute-start.10
  153.1 6.4 collective-permute-start.11
  159.6 6.6 %collective-permute-start.12 = (f32[3,64,128]{2,1,0:T(8,128)S(1)}, f32[3,64,128]{2,1,0:T(8,128)S(1)}, u32[]{:S(2)}, u32[]{:S(2)}) collective-permute-start(f32[3,64,128]{2,1,0:T(8,128)S(1)} %get-tuple-element.35), channel_id=1, source_target_pairs={{0,144},{16,160},{32,176},{48,192},{64,208},{80,224},{96,240},{112... | collective-permute-start | bytes 294920 | tf_op jit(solution)/shard_map/ppermute | solution.py:32
  166.3 9.4 %collective-permute-start.13 = (f32[3,64,128]{2,1,0:T(8,128)S(1)}, f32[3,64,128]{2,1,0:T(8,128)S(1)}, u32[]{:S(2)}, u32[]{:S(2)}) collective-permute-start(f32[3,64,128]{2,1,0:T(8,128)S(1)} %get-tuple-element.34), channel_id=1, source_target_pairs={{0,160},{16,176},{32,192},{48,208},{64,224},{80,240},{96,0},{112,1... | collective-permute-start | bytes 294920 | tf_op jit(solution)/shard_map/ppermute | solution.py:32
  178.5 12.1 %collective-permute-start.15 = (f32[3,64,128]{2,1,0:T(8,128)S(1)}, f32[3,64,128]{2,1,0:T(8,128)S(1)}, u32[]{:S(2)}, u32[]{:S(2)}) collective-permute-start(f32[3,64,128]{2,1,0:T(8,128)S(1)} %get-tuple-element.32), channel_id=1, source_target_pairs={{0,192},{16,208},{32,224},{48,240},{64,0},{80,16},{96,32},{112,48}... | collective-permute-start | bytes 294920 | tf_op jit(solution)/shard_map/ppermute | solution.py:32
  200.1 6.9 %collective-permute-start.18 = (f32[3,64,128]{2,1,0:T(8,128)S(1)}, f32[3,64,128]{2,1,0:T(8,128)S(1)}, u32[]{:S(2)}, u32[]{:S(2)}) collective-permute-start(f32[3,64,128]{2,1,0:T(8,128)S(1)} %get-tuple-element.29), channel_id=1, source_target_pairs={{0,240},{16,0},{32,16},{48,32},{64,48},{80,64},{96,80},{112,96},{1... | collective-permute-start | bytes 294920 | tf_op jit(solution)/shard_map/ppermute | solution.py:32
  209.9 9.1 %collective-permute-done.15 = f32[3,64,128]{2,1,0:T(8,128)S(1)} collective-permute-done((f32[3,64,128]{2,1,0:T(8,128)S(1)}, f32[3,64,128]{2,1,0:T(8,128)S(1)}, u32[]{:S(2)}, u32[]{:S(2)}) %collective-permute-start.15) | collective-permute-done | bytes 98336 | tf_op jit(solution)/shard_map/ppermute | solution.py:32
  219.0 5.4 collective-permute-done.16
  232.7 6.3 all-to-all-start.1
  239.0 22.0 %all-to-all-done.1 = f32[48,64,128]{2,1,0:T(8,128)S(1)} async-done(((f32[48,64,128]{2,1,0:T(8,128)}), f32[48,64,128]{2,1,0:T(8,128)S(1)}, u32[]{:S(2)}, u32[]{:S(2)}) %all-to-all-start.1) | async-done | bytes 1572896 | tf_op jit(solution)/shard_map/all_to_all | solution.py:142
  272.1 5.4 reshape.214
  277.5 24.6 %all_to_all.93 = f32[16,1,24576]{2,1,0:T(1,128)S(1)} all-to-all(f32[16,1,24576]{2,1,0:T(1,128)S(1)} %reshape.214), channel_id=1, replica_groups=mesh['phys'=2,'gx'=16,'gy'=16] {'gy'}, dimensions={0} | all-to-all | bytes 3145728 | tf_op jit(solution)/shard_map/all_to_all | solution.py:140
  320.6 32.6 %collective-permute-done.19 = f32[48,64,128]{2,1,0:T(8,128)S(1)} collective-permute-done((f32[48,64,128]{2,1,0:T(8,128)S(1)}, f32[48,64,128]{2,1,0:T(8,128)S(1)}, u32[]{:S(2)}, u32[]{:S(2)}) %collective-permute-start.19) | collective-permute-done | bytes 1572896 | tf_op jit(solution)/shard_map/ppermute | solution.py:63
  359.3 74.2 %all_to_all.94 = f32[48,64,128]{2,1,0:T(8,128)S(1)} all-to-all(f32[48,64,128]{2,1,0:T(8,128)S(1)} %reshape.186), channel_id=1, replica_groups=mesh['phys'=2,'gx'=16,'gy'=16] {'gx'}, dimensions={0} | all-to-all | bytes 3145728 | tf_op jit(solution)/shard_map/all_to_all | solution.py:132
  464.4 7.7 %collective-permute-start.25 = (f32[3,64,128]{2,1,0:T(8,128)S(1)}, f32[3,64,128]{2,1,0:T(8,128)S(1)}, u32[]{:S(2)}, u32[]{:S(2)}) collective-permute-start(f32[3,64,128]{2,1,0:T(8,128)S(1)} %get-tuple-element.19), channel_id=1, source_target_pairs={{0,96},{16,112},{32,128},{48,144},{64,160},{80,176},{96,192},{112,... | collective-permute-start | bytes 294920 | tf_op jit(solution)/shard_map/ppermute | solution.py:32
  482.4 8.0 %collective-permute-start.28 = (f32[3,64,128]{2,1,0:T(8,128)S(1)}, f32[3,64,128]{2,1,0:T(8,128)S(1)}, u32[]{:S(2)}, u32[]{:S(2)}) collective-permute-start(f32[3,64,128]{2,1,0:T(8,128)S(1)} %get-tuple-element.16), channel_id=1, source_target_pairs={{0,144},{16,160},{32,176},{48,192},{64,208},{80,224},{96,240},{112... | collective-permute-start | bytes 294920 | tf_op jit(solution)/shard_map/ppermute | solution.py:32
  490.4 8.4 %collective-permute-start.29 = (f32[3,64,128]{2,1,0:T(8,128)S(1)}, f32[3,64,128]{2,1,0:T(8,128)S(1)}, u32[]{:S(2)}, u32[]{:S(2)}) collective-permute-start(f32[3,64,128]{2,1,0:T(8,128)S(1)} %get-tuple-element.15), channel_id=1, source_target_pairs={{0,160},{16,176},{32,192},{48,208},{64,224},{80,240},{96,0},{112,1... | collective-permute-start | bytes 294920 | tf_op jit(solution)/shard_map/ppermute | solution.py:32
  500.9 6.5 collective-permute-done.26
  509.3 14.0 %collective-permute-done.27 = f32[3,64,128]{2,1,0:T(8,128)S(1)} collective-permute-done((f32[3,64,128]{2,1,0:T(8,128)S(1)}, f32[3,64,128]{2,1,0:T(8,128)S(1)}, u32[]{:S(2)}, u32[]{:S(2)}) %collective-permute-start.27) | collective-permute-done | bytes 98336 | tf_op jit(solution)/shard_map/ppermute | solution.py:32
  530.8 5.6 collective-permute-done.30
  536.3 7.0 %collective-permute-done.31 = f32[3,64,128]{2,1,0:T(8,128)S(1)} collective-permute-done((f32[3,64,128]{2,1,0:T(8,128)S(1)}, f32[3,64,128]{2,1,0:T(8,128)S(1)}, u32[]{:S(2)}, u32[]{:S(2)}) %collective-permute-start.31) | collective-permute-done | bytes 98336 | tf_op jit(solution)/shard_map/ppermute | solution.py:32
  544.7 8.5 %collective-permute-done.33 = f32[3,64,128]{2,1,0:T(8,128)S(1)} collective-permute-done((f32[3,64,128]{2,1,0:T(8,128)S(1)}, f32[3,64,128]{2,1,0:T(8,128)S(1)}, u32[]{:S(2)}, u32[]{:S(2)}) %collective-permute-start.33) | collective-permute-done | bytes 98336 | tf_op jit(solution)/shard_map/ppermute | solution.py:32
  555.9 26.4 %all_to_all.95 = f32[48,64,128]{2,1,0:T(8,128)S(1)} all-to-all(f32[48,64,128]{2,1,0:T(8,128)S(1)} %bitcast.255), channel_id=1, replica_groups=mesh['phys'=2,'gx'=16,'gy'=16] {'gy'}, dimensions={0} | all-to-all | bytes 3145728 | tf_op jit(solution)/shard_map/all_to_all | solution.py:142
  593.5 5.4 reshape.216
  598.9 24.9 %all_to_all.96 = f32[16,1,24576]{2,1,0:T(1,128)S(1)} all-to-all(f32[16,1,24576]{2,1,0:T(1,128)S(1)} %reshape.216), channel_id=1, replica_groups=mesh['phys'=2,'gx'=16,'gy'=16] {'gy'}, dimensions={0} | all-to-all | bytes 3145728 | tf_op jit(solution)/shard_map/all_to_all | solution.py:140
  642.2 5.4 collective-permute-start.37
  651.3 6.5 collective-permute-done.38
  (166 shorter events, 190.7 us)
Async XLA Ops:
  25.3 85.4 %all-to-all-start = ((f32[48,64,128]{2,1,0:T(8,128)}), f32[48,64,128]{2,1,0:T(8,128)S(1)}, u32[]{:S(2)}, u32[]{:S(2)}) async-start(f32[48,64,128]{2,1,0:T(8,128)} %reshape.181), calls=%async_computation | async-start | bytes 3145728 | tf_op jit(solution)/shard_map/all_to_all | solution.py:132
  117.5 21.6 %collective-permute-start.4 = (f32[3,64,128]{2,1,0:T(8,128)S(1)}, f32[3,64,128]{2,1,0:T(8,128)S(1)}, u32[]{:S(2)}, u32[]{:S(2)}) collective-permute-start(f32[3,64,128]{2,1,0:T(8,128)S(1)} %get-tuple-element.43), channel_id=1, source_target_pairs={{0,16},{16,32},{32,48},{48,64},{64,80},{80,96},{96,112},{112,128},... | collective-permute-start | bytes 294920 | tf_op jit(solution)/shard_map/ppermute | solution.py:32
  120.4 27.1 %collective-permute-start.5 = (f32[3,64,128]{2,1,0:T(8,128)S(1)}, f32[3,64,128]{2,1,0:T(8,128)S(1)}, u32[]{:S(2)}, u32[]{:S(2)}) collective-permute-start(f32[3,64,128]{2,1,0:T(8,128)S(1)} %get-tuple-element.42), channel_id=1, source_target_pairs={{0,32},{16,48},{32,64},{48,80},{64,96},{80,112},{96,128},{112,144}... | collective-permute-start | bytes 294920 | tf_op jit(solution)/shard_map/ppermute | solution.py:32
  125.1 28.1 %collective-permute-start.6 = (f32[3,64,128]{2,1,0:T(8,128)S(1)}, f32[3,64,128]{2,1,0:T(8,128)S(1)}, u32[]{:S(2)}, u32[]{:S(2)}) collective-permute-start(f32[3,64,128]{2,1,0:T(8,128)S(1)} %get-tuple-element.41), channel_id=1, source_target_pairs={{0,48},{16,64},{32,80},{48,96},{64,112},{80,128},{96,144},{112,160... | collective-permute-start | bytes 294920 | tf_op jit(solution)/shard_map/ppermute | solution.py:32
  131.0 28.6 %collective-permute-start.7 = (f32[3,64,128]{2,1,0:T(8,128)S(1)}, f32[3,64,128]{2,1,0:T(8,128)S(1)}, u32[]{:S(2)}, u32[]{:S(2)}) collective-permute-start(f32[3,64,128]{2,1,0:T(8,128)S(1)} %get-tuple-element.40), channel_id=1, source_target_pairs={{0,64},{16,80},{32,96},{48,112},{64,128},{80,144},{96,160},{112,17... | collective-permute-start | bytes 294920 | tf_op jit(solution)/shard_map/ppermute | solution.py:32
  137.1 29.2 %collective-permute-start.8 = (f32[3,64,128]{2,1,0:T(8,128)S(1)}, f32[3,64,128]{2,1,0:T(8,128)S(1)}, u32[]{:S(2)}, u32[]{:S(2)}) collective-permute-start(f32[3,64,128]{2,1,0:T(8,128)S(1)} %get-tuple-element.39), channel_id=1, source_target_pairs={{0,80},{16,96},{32,112},{48,128},{64,144},{80,160},{96,176},{112,1... | collective-permute-start | bytes 294920 | tf_op jit(solution)/shard_map/ppermute | solution.py:32
  139.1 36.6 %collective-permute-start.9 = (f32[3,64,128]{2,1,0:T(8,128)S(1)}, f32[3,64,128]{2,1,0:T(8,128)S(1)}, u32[]{:S(2)}, u32[]{:S(2)}) collective-permute-start(f32[3,64,128]{2,1,0:T(8,128)S(1)} %get-tuple-element.38), channel_id=1, source_target_pairs={{0,96},{16,112},{32,128},{48,144},{64,160},{80,176},{96,192},{112,... | collective-permute-start | bytes 294920 | tf_op jit(solution)/shard_map/ppermute | solution.py:32
  147.6 31.0 %collective-permute-start.10 = (f32[3,64,128]{2,1,0:T(8,128)S(1)}, f32[3,64,128]{2,1,0:T(8,128)S(1)}, u32[]{:S(2)}, u32[]{:S(2)}) collective-permute-start(f32[3,64,128]{2,1,0:T(8,128)S(1)} %get-tuple-element.37), channel_id=1, source_target_pairs={{0,112},{16,128},{32,144},{48,160},{64,176},{80,192},{96,208},{112... | collective-permute-start | bytes 294920 | tf_op jit(solution)/shard_map/ppermute | solution.py:32
  153.1 37.6 %collective-permute-start.11 = (f32[3,64,128]{2,1,0:T(8,128)S(1)}, f32[3,64,128]{2,1,0:T(8,128)S(1)}, u32[]{:S(2)}, u32[]{:S(2)}) collective-permute-start(f32[3,64,128]{2,1,0:T(8,128)S(1)} %get-tuple-element.36), channel_id=1, source_target_pairs={{0,128},{16,144},{32,160},{48,176},{64,192},{80,208},{96,224},{112... | collective-permute-start | bytes 294920 | tf_op jit(solution)/shard_map/ppermute | solution.py:32
  159.6 36.3 %collective-permute-start.12 = (f32[3,64,128]{2,1,0:T(8,128)S(1)}, f32[3,64,128]{2,1,0:T(8,128)S(1)}, u32[]{:S(2)}, u32[]{:S(2)}) collective-permute-start(f32[3,64,128]{2,1,0:T(8,128)S(1)} %get-tuple-element.35), channel_id=1, source_target_pairs={{0,144},{16,160},{32,176},{48,192},{64,208},{80,224},{96,240},{112... | collective-permute-start | bytes 294920 | tf_op jit(solution)/shard_map/ppermute | solution.py:32
  166.3 33.8 %collective-permute-start.13 = (f32[3,64,128]{2,1,0:T(8,128)S(1)}, f32[3,64,128]{2,1,0:T(8,128)S(1)}, u32[]{:S(2)}, u32[]{:S(2)}) collective-permute-start(f32[3,64,128]{2,1,0:T(8,128)S(1)} %get-tuple-element.34), channel_id=1, source_target_pairs={{0,160},{16,176},{32,192},{48,208},{64,224},{80,240},{96,0},{112,1... | collective-permute-start | bytes 294920 | tf_op jit(solution)/shard_map/ppermute | solution.py:32
  175.7 34.2 %collective-permute-start.14 = (f32[3,64,128]{2,1,0:T(8,128)S(1)}, f32[3,64,128]{2,1,0:T(8,128)S(1)}, u32[]{:S(2)}, u32[]{:S(2)}) collective-permute-start(f32[3,64,128]{2,1,0:T(8,128)S(1)} %get-tuple-element.33), channel_id=1, source_target_pairs={{0,176},{16,192},{32,208},{48,224},{64,240},{80,0},{96,16},{112,32... | collective-permute-start | bytes 294920 | tf_op jit(solution)/shard_map/ppermute | solution.py:32
  178.5 40.5 %collective-permute-start.15 = (f32[3,64,128]{2,1,0:T(8,128)S(1)}, f32[3,64,128]{2,1,0:T(8,128)S(1)}, u32[]{:S(2)}, u32[]{:S(2)}) collective-permute-start(f32[3,64,128]{2,1,0:T(8,128)S(1)} %get-tuple-element.32), channel_id=1, source_target_pairs={{0,192},{16,208},{32,224},{48,240},{64,0},{80,16},{96,32},{112,48}... | collective-permute-start | bytes 294920 | tf_op jit(solution)/shard_map/ppermute | solution.py:32
  190.7 33.7 %collective-permute-start.16 = (f32[3,64,128]{2,1,0:T(8,128)S(1)}, f32[3,64,128]{2,1,0:T(8,128)S(1)}, u32[]{:S(2)}, u32[]{:S(2)}) collective-permute-start(f32[3,64,128]{2,1,0:T(8,128)S(1)} %get-tuple-element.31), channel_id=1, source_target_pairs={{0,208},{16,224},{32,240},{48,0},{64,16},{80,32},{96,48},{112,64},... | collective-permute-start | bytes 294920 | tf_op jit(solution)/shard_map/ppermute | solution.py:32
  195.9 32.7 %collective-permute-start.17 = (f32[3,64,128]{2,1,0:T(8,128)S(1)}, f32[3,64,128]{2,1,0:T(8,128)S(1)}, u32[]{:S(2)}, u32[]{:S(2)}) collective-permute-start(f32[3,64,128]{2,1,0:T(8,128)S(1)} %get-tuple-element.30), channel_id=1, source_target_pairs={{0,224},{16,240},{32,0},{48,16},{64,32},{80,48},{96,64},{112,80},{... | collective-permute-start | bytes 294920 | tf_op jit(solution)/shard_map/ppermute | solution.py:32
  200.1 30.8 %collective-permute-start.18 = (f32[3,64,128]{2,1,0:T(8,128)S(1)}, f32[3,64,128]{2,1,0:T(8,128)S(1)}, u32[]{:S(2)}, u32[]{:S(2)}) collective-permute-start(f32[3,64,128]{2,1,0:T(8,128)S(1)} %get-tuple-element.29), channel_id=1, source_target_pairs={{0,240},{16,0},{32,16},{48,32},{64,48},{80,64},{96,80},{112,96},{1... | collective-permute-start | bytes 294920 | tf_op jit(solution)/shard_map/ppermute | solution.py:32
  232.7 28.3 %all-to-all-start.1 = ((f32[48,64,128]{2,1,0:T(8,128)}), f32[48,64,128]{2,1,0:T(8,128)S(1)}, u32[]{:S(2)}, u32[]{:S(2)}) async-start(f32[48,64,128]{2,1,0:T(8,128)} %bitcast.50), calls=%async_computation.1 | async-start | bytes 3145728 | tf_op jit(solution)/shard_map/all_to_all | solution.py:142
  314.0 39.2 %collective-permute-start.19 = (f32[48,64,128]{2,1,0:T(8,128)S(1)}, f32[48,64,128]{2,1,0:T(8,128)S(1)}, u32[]{:S(2)}, u32[]{:S(2)}) collective-permute-start(f32[48,64,128]{2,1,0:T(8,128)S(1)} %bitcast.253), channel_id=1, source_target_pairs={{0,256},{256,0},{1,257},{257,1},{2,258},{258,2},{3,259},{259,3},{4... | collective-permute-start | bytes 4718600 | tf_op jit(solution)/shard_map/ppermute | solution.py:63
  440.3 24.1 %collective-permute-start.20 = (f32[3,64,128]{2,1,0:T(8,128)S(1)}, f32[3,64,128]{2,1,0:T(8,128)S(1)}, u32[]{:S(2)}, u32[]{:S(2)}) collective-permute-start(f32[3,64,128]{2,1,0:T(8,128)S(1)} %get-tuple-element.24), channel_id=1, source_target_pairs={{0,16},{16,32},{32,48},{48,64},{64,80},{80,96},{96,112},{112,128},... | collective-permute-start | bytes 294920 | tf_op jit(solution)/shard_map/ppermute | solution.py:32
  445.3 26.8 %collective-permute-start.21 = (f32[3,64,128]{2,1,0:T(8,128)S(1)}, f32[3,64,128]{2,1,0:T(8,128)S(1)}, u32[]{:S(2)}, u32[]{:S(2)}) collective-permute-start(f32[3,64,128]{2,1,0:T(8,128)S(1)} %get-tuple-element.23), channel_id=1, source_target_pairs={{0,32},{16,48},{32,64},{48,80},{64,96},{80,112},{96,128},{112,144}... | collective-permute-start | bytes 294920 | tf_op jit(solution)/shard_map/ppermute | solution.py:32
  450.2 27.1 %collective-permute-start.22 = (f32[3,64,128]{2,1,0:T(8,128)S(1)}, f32[3,64,128]{2,1,0:T(8,128)S(1)}, u32[]{:S(2)}, u32[]{:S(2)}) collective-permute-start(f32[3,64,128]{2,1,0:T(8,128)S(1)} %get-tuple-element.22), channel_id=1, source_target_pairs={{0,48},{16,64},{32,80},{48,96},{64,112},{80,128},{96,144},{112,160... | collective-permute-start | bytes 294920 | tf_op jit(solution)/shard_map/ppermute | solution.py:32
  455.5 26.9 %collective-permute-start.23 = (f32[3,64,128]{2,1,0:T(8,128)S(1)}, f32[3,64,128]{2,1,0:T(8,128)S(1)}, u32[]{:S(2)}, u32[]{:S(2)}) collective-permute-start(f32[3,64,128]{2,1,0:T(8,128)S(1)} %get-tuple-element.21), channel_id=1, source_target_pairs={{0,64},{16,80},{32,96},{48,112},{64,128},{80,144},{96,160},{112,17... | collective-permute-start | bytes 294920 | tf_op jit(solution)/shard_map/ppermute | solution.py:32
  460.0 30.5 %collective-permute-start.24 = (f32[3,64,128]{2,1,0:T(8,128)S(1)}, f32[3,64,128]{2,1,0:T(8,128)S(1)}, u32[]{:S(2)}, u32[]{:S(2)}) collective-permute-start(f32[3,64,128]{2,1,0:T(8,128)S(1)} %get-tuple-element.20), channel_id=1, source_target_pairs={{0,80},{16,96},{32,112},{48,128},{64,144},{80,160},{96,176},{112,1... | collective-permute-start | bytes 294920 | tf_op jit(solution)/shard_map/ppermute | solution.py:32
  464.4 34.6 %collective-permute-start.25 = (f32[3,64,128]{2,1,0:T(8,128)S(1)}, f32[3,64,128]{2,1,0:T(8,128)S(1)}, u32[]{:S(2)}, u32[]{:S(2)}) collective-permute-start(f32[3,64,128]{2,1,0:T(8,128)S(1)} %get-tuple-element.19), channel_id=1, source_target_pairs={{0,96},{16,112},{32,128},{48,144},{64,160},{80,176},{96,192},{112,... | collective-permute-start | bytes 294920 | tf_op jit(solution)/shard_map/ppermute | solution.py:32
  472.1 35.3 %collective-permute-start.26 = (f32[3,64,128]{2,1,0:T(8,128)S(1)}, f32[3,64,128]{2,1,0:T(8,128)S(1)}, u32[]{:S(2)}, u32[]{:S(2)}) collective-permute-start(f32[3,64,128]{2,1,0:T(8,128)S(1)} %get-tuple-element.18), channel_id=1, source_target_pairs={{0,112},{16,128},{32,144},{48,160},{64,176},{80,192},{96,208},{112... | collective-permute-start | bytes 294920 | tf_op jit(solution)/shard_map/ppermute | solution.py:32
  477.3 46.0 %collective-permute-start.27 = (f32[3,64,128]{2,1,0:T(8,128)S(1)}, f32[3,64,128]{2,1,0:T(8,128)S(1)}, u32[]{:S(2)}, u32[]{:S(2)}) collective-permute-start(f32[3,64,128]{2,1,0:T(8,128)S(1)} %get-tuple-element.17), channel_id=1, source_target_pairs={{0,128},{16,144},{32,160},{48,176},{64,192},{80,208},{96,224},{112... | collective-permute-start | bytes 294920 | tf_op jit(solution)/shard_map/ppermute | solution.py:32
  482.4 42.8 %collective-permute-start.28 = (f32[3,64,128]{2,1,0:T(8,128)S(1)}, f32[3,64,128]{2,1,0:T(8,128)S(1)}, u32[]{:S(2)}, u32[]{:S(2)}) collective-permute-start(f32[3,64,128]{2,1,0:T(8,128)S(1)} %get-tuple-element.16), channel_id=1, source_target_pairs={{0,144},{16,160},{32,176},{48,192},{64,208},{80,224},{96,240},{112... | collective-permute-start | bytes 294920 | tf_op jit(solution)/shard_map/ppermute | solution.py:32
  490.4 36.7 %collective-permute-start.29 = (f32[3,64,128]{2,1,0:T(8,128)S(1)}, f32[3,64,128]{2,1,0:T(8,128)S(1)}, u32[]{:S(2)}, u32[]{:S(2)}) collective-permute-start(f32[3,64,128]{2,1,0:T(8,128)S(1)} %get-tuple-element.15), channel_id=1, source_target_pairs={{0,160},{16,176},{32,192},{48,208},{64,224},{80,240},{96,0},{112,1... | collective-permute-start | bytes 294920 | tf_op jit(solution)/shard_map/ppermute | solution.py:32
  498.9 37.4 %collective-permute-start.30 = (f32[3,64,128]{2,1,0:T(8,128)S(1)}, f32[3,64,128]{2,1,0:T(8,128)S(1)}, u32[]{:S(2)}, u32[]{:S(2)}) collective-permute-start(f32[3,64,128]{2,1,0:T(8,128)S(1)} %get-tuple-element.14), channel_id=1, source_target_pairs={{0,176},{16,192},{32,208},{48,224},{64,240},{80,0},{96,16},{112,32... | collective-permute-start | bytes 294920 | tf_op jit(solution)/shard_map/ppermute | solution.py:32
  507.4 36.0 %collective-permute-start.31 = (f32[3,64,128]{2,1,0:T(8,128)S(1)}, f32[3,64,128]{2,1,0:T(8,128)S(1)}, u32[]{:S(2)}, u32[]{:S(2)}) collective-permute-start(f32[3,64,128]{2,1,0:T(8,128)S(1)} %get-tuple-element.13), channel_id=1, source_target_pairs={{0,192},{16,208},{32,224},{48,240},{64,0},{80,16},{96,32},{112,48}... | collective-permute-start | bytes 294920 | tf_op jit(solution)/shard_map/ppermute | solution.py:32
  525.2 28.0 %collective-permute-start.33 = (f32[3,64,128]{2,1,0:T(8,128)S(1)}, f32[3,64,128]{2,1,0:T(8,128)S(1)}, u32[]{:S(2)}, u32[]{:S(2)}) collective-permute-start(f32[3,64,128]{2,1,0:T(8,128)S(1)} %get-tuple-element.11), channel_id=1, source_target_pairs={{0,224},{16,240},{32,0},{48,16},{64,32},{80,48},{96,64},{112,80},{... | collective-permute-start | bytes 294920 | tf_op jit(solution)/shard_map/ppermute | solution.py:32
  527.2 27.9 %collective-permute-start.34 = (f32[3,64,128]{2,1,0:T(8,128)S(1)}, f32[3,64,128]{2,1,0:T(8,128)S(1)}, u32[]{:S(2)}, u32[]{:S(2)}) collective-permute-start(f32[3,64,128]{2,1,0:T(8,128)S(1)} %get-tuple-element.10), channel_id=1, source_target_pairs={{0,240},{16,0},{32,16},{48,32},{64,48},{80,64},{96,80},{112,96},{1... | collective-permute-start | bytes 294920 | tf_op jit(solution)/shard_map/ppermute | solution.py:32
  (12 other events, 289.7 us)
